TPU v7x, 128 devices: a whole 4x4x4 slice. The times are simulated.
128 devices in a mesh: blk: 32 (over z, x, y_lo), grp: 4 (over y_hi, core).
Axes of the slice: x: 4, y: 4 (y_hi: 2, y_lo: 2; y = y_hi * 2 + y_lo), z: 4, core: 2. Of those that a mesh axis runs over, the one named last changes fastest.
Arguments:
- queries: bfloat16 [2048, 2048], P(('blk', 'grp')), may hold values from -0.125 to 0.125
- training: bfloat16 [131072, 2048], P(('blk', 'grp')), may hold values from -24 to 24
Outputs:
- scores: float32 [2048, 131072], P(None, ('blk', 'grp'))
- gram: float32 [2048, 2048], P(('blk', 'grp'))
All inputs are finite; a program needn't handle non-finite values.
Results may differ from a plain program's by a relative error of at most 0.0003.
Values may be sent and summed in bfloat16 or wider, within the bound.
A program may use at most 128 MiB of HBM per device.

v0:
```python
import functools

import jax
import jax.numpy as jnp
from jax import lax
from jax.experimental import pallas as pl
from jax.experimental.pallas import tpu as pltpu
from jax.sharding import PartitionSpec as P

MESH = pl.DeviceIdType.MESH
ALL = pl.ds(0, 4)
AXES = ("z", "x", "y")
B = 128
CH = 136
AG_PARTS = (((0, 640), "yxz"), ((640, 1280), "zyx"), ((1280, 2048), "xzy"))
RS_PARTS = (((0, 48), "zxy"), ((48, 96), "xyz"), ((96, 136), "yzx"))
N_SEM = 192
HERE = 3
STAGES = (2, 1, 3, 0)
ORDER = (
    "gather",
    "share 0",
    "share 1",
    "gram 2",
    "share 2",
    "join 0",
    "gather",
    "join 1",
    "gram 3",
    "share 3",
    "pass 0",
    "join 2",
    "pass 1",
    "join 3",
    "pass 2",
    "pass 3",
    "gather",
    "reduce",
    "gather",
    "reduce",
    "gather",
    "gather",
    "reduce",
    "exchange",
    "scores 0",
    "scores 1",
    "scores 2",
)


def stored(axis, i):
    return lax.rem(i, 2) * 2 + lax.div(i, 2) if axis == "y" else i


class Net:
    def __init__(self, ssem, rsem):
        blk, grp = lax.axis_index("blk"), lax.axis_index("grp")
        self.at = {
            "z": lax.div(blk, 8),
            "x": lax.rem(lax.div(blk, 2), 4),
            "y": lax.div(grp, 2) * 2 + lax.rem(blk, 2),
        }
        self.core = lax.rem(grp, 2)
        self.group = lax.div(blk, 2)
        self.k = lax.rem(blk, 2) * 4 + grp
        self.ssem, self.rsem = ssem, rsem
        self.count = 0
        self.sent = []

    def device(self, core=None, **moved):
        at = {**self.at, **moved}
        core = self.core if core is None else core
        return (at["z"] * 8 + at["x"] * 2 + lax.rem(at["y"], 2), lax.div(at["y"], 2) * 2 + core)

    def hop(self, axis, by):
        return lax.rem(self.at[axis] + by + 4, 4)

    def neighbour(self, axis, by):
        return self.device(**{axis: self.hop(axis, by)})

    def sibling(self):
        return self.device(core=1 - self.core)

    def send(self, src, dst, to):
        t = self.count
        self.count += 1
        copy = pltpu.make_async_remote_copy(
            src_ref=src,
            dst_ref=dst,
            send_sem=self.ssem.at[t],
            recv_sem=self.rsem.at[t],
            device_id=to,
            device_id_type=MESH,
        )
        copy.start()
        self.sent.append(copy)
        return copy


def member(group, k):
    return (group * 2 + lax.div(k, 4), lax.rem(k, 4))


def gather_part(net, q, cols, order):
    lo, hi = cols

    def region(idx, c=None):
        at = [idx[a] for a in AXES]
        return q.at[at[0], at[1], at[2], net.core, :, pl.ds(lo, hi - lo)] if c is None else q.at[
            at[0], at[1], at[2], net.core, :, pl.ds(*c)
        ]

    def halves(idx):
        free = [a for a in AXES if isinstance(idx[a], pl.Slice)]
        if free:
            return [region({**idx, free[0]: pl.ds(2 * h, 2)}) for h in range(2)]
        mid = (hi - lo) // 256 * 128
        return [region(idx, (lo, mid)), region(idx, (lo + mid, hi - lo - mid))]

    idx = {a: stored(a, net.at[a]) for a in AXES}
    to_sibling = []

    def spread(axis):
        here = region(idx)
        return [net.send(here, here, net.neighbour(axis, by)) for by in (2, 1, -1)]

    def ahead(at):
        here = region(at)
        return [net.send(here, here, net.neighbour(order[2], by)) for by in (1, -1)]

    def hand(at):
        to_sibling.append(net.send(region(at), region(at), net.sibling()))

    first = spread(order[0])
    yield
    for copy in first:
        copy.wait_recv()
    idx = {**idx, order[0]: ALL}
    second = spread(order[1])
    third = [ahead(idx)]
    hand(idx)
    yield
    for copy in second:
        copy.wait_recv()
    for by in (1, -1, 2):
        at = {**idx, order[1]: stored(order[1], net.hop(order[1], by))}
        third.append(ahead(at))
        hand(at)
    yield
    idx = {**idx, order[1]: ALL}
    axis = order[2]
    low, high, far = ({**idx, axis: stored(axis, net.hop(axis, by))} for by in (-1, 1, 2))
    for up, _ in third:
        up.wait_recv()
    src = halves(low)[0]
    on_up = net.send(src, src, net.neighbour(axis, 1))
    for _, down in third:
        down.wait_recv()
    src = halves(high)[1]
    on_down = net.send(src, src, net.neighbour(axis, -1))
    hand(low)
    hand(high)
    yield
    on_up.wait_recv()
    on_down.wait_recv()
    hand(far)
    yield
    for copy in to_sibling:
        copy.wait_recv()


class Reduce:
    def __init__(self, net, p, bufs, rows, order):
        self.net, self.p, self.bufs, self.rows, self.order = net, p, bufs, rows, order
        self.up, self.down = net.neighbour(order[0], 1), net.neighbour(order[0], -1)
        self.copies = {}

    def region(self, idx):
        lo, hi = self.rows
        at = [idx[a] for a in AXES]
        return self.p.at[at[0], at[1], at[2], self.net.core, pl.ds(lo, hi - lo)]

    def halves(self, stage, by):
        first = self.order[0]
        if first == "z":
            idx = {"z": self.net.hop("z", by), "x": ALL, "y": ALL}
        else:
            idx = {"x": ALL, "y": ALL, "z": self.net.hop("z", STAGES[stage])}
            idx[first] = stored(first, self.net.hop(first, by))
        free = next(a for a in AXES if isinstance(idx[a], pl.Slice))
        return [self.region({**idx, free: pl.ds(2 * h, 2)}) for h in range(2)]

    def go(self, stage, name, src, slot, to):
        dst = self.bufs[0][slot]
        if self.order[0] != "z":
            dst = dst.at[stage]
        self.copies[stage, name] = self.net.send(src, dst, to), dst

    def start(self, stage):
        whole = self.order[0] != "z"
        if whole or STAGES[stage] == 2:
            far = self.halves(stage, 2)
            self.go(stage, "via_up", far[0], 0, self.up)
            self.go(stage, "via_down", far[1], 1, self.down)
        if whole or STAGES[stage] == 1:
            self.go(stage, "own_up", self.halves(stage, 1)[1], 2, self.up)
        if whole or STAGES[stage] == 3:
            self.go(stage, "own_down", self.halves(stage, -1)[0], 3, self.down)

    def add(self, stage, name, ref):
        copy, dst = self.copies[stage, name]
        copy.wait_recv()
        ref[...] += dst[...]

    def pass_on(self, stage):
        whole = self.order[0] != "z"
        via = stage if whole else STAGES.index(2)
        if whole or STAGES[stage] == 1:
            high = self.halves(stage, 1)[0]
            self.add(via, "via_up", high)
            self.go(stage, "sum_up", high, 4, self.up)
        if whole or STAGES[stage] == 3:
            low = self.halves(stage, -1)[1]
            self.add(via, "via_down", low)
            self.go(stage, "sum_down", low, 5, self.down)

    def rest(self):
        net, order = self.net, self.order
        whole = order[0] != "z"
        for stage in range(4) if whole else (None,):
            mine = self.halves(stage, 0)
            for name, h, at in (
                ("own_up", 1, STAGES.index(1)),
                ("sum_down", 1, STAGES.index(3)),
                ("own_down", 0, STAGES.index(3)),
                ("sum_up", 0, STAGES.index(1)),
            ):
                self.add(stage if whole else at, name, mine[h])
        idx = {**{a: ALL for a in AXES}, order[0]: stored(order[0], net.at[order[0]])}
        for axis, buf in zip(order[1:], self.bufs[1:], strict=True):
            copies = [
                net.send(
                    self.region({**idx, axis: stored(axis, net.hop(axis, by))}),
                    buf[i],
                    net.neighbour(axis, by),
                )
                for i, by in enumerate((2, 1, -1))
            ]
            idx = {**idx, axis: stored(axis, net.at[axis])}
            yield
            for copy in copies:
                copy.wait_recv()
            self.region(idx)[...] += buf[0][...] + buf[1][...] + buf[2][...]


def part_buffers(rows, order):
    n = rows[1] - rows[0]
    return [[(2, 4, n, B) if order[0] == "z" else (4, 2, n, B)] * 6, [(4, n, B)] * 3, [(n, B)] * 3]


def step_all(gens):
    left = False
    for g in list(gens):
        try:
            next(g)
            left = True
        except StopIteration:
            gens.remove(g)
    return left


def kernel(scale, *refs):
    (q_in, t_in, s, g_out, q, t, p, d2d, x, slots) = refs[:10]
    *flat, ssem, rsem, xsem, lsem = refs[10:]
    flat = iter(flat)
    bufs = [[[next(flat) for _ in shapes] for shapes in part_buffers(*part)] for part in RS_PARTS]
    net = Net(ssem, rsem)
    zi, xi, yi = (stored(a, net.at[a]) for a in AXES)
    core, group, k = net.core, net.group, net.k
    odd = lax.rem(group, 2)
    packed = jnp.logical_and(k == 0, odd != lax.div(group, 8))
    other = jnp.where(
        packed, group + 1 - 2 * odd, lax.rem(group + jnp.where(k == 0, 8, k), 16)
    )

    load_q = pltpu.make_async_copy(q_in, q.at[zi, xi, yi, core], lsem.at[0])
    load_q.start()
    load_t = pltpu.make_async_copy(t_in, t, lsem.at[1])
    load_t.start()

    barrier = pltpu.get_barrier_semaphore()

    def greet(device):
        pl.semaphore_signal(barrier, inc=1, device_id=device, device_id_type=MESH)

    for axis in AXES:
        greet(net.neighbour(axis, 1))
        greet(net.neighbour(axis, -1))
        greet(net.neighbour(axis, 2))
    greet(net.sibling())
    load_t.wait()

    p[:, :, :, :, pl.ds(B, 8)] = jnp.zeros((4, 4, 4, 2, 8, B), jnp.float32)
    row = lax.broadcasted_iota(jnp.int32, (B, B), 0)
    col = lax.broadcasted_iota(jnp.int32, (B, B), 1)

    def chunk(g, kk):
        return p.at[lax.div(g, 4), lax.rem(g, 4), kk // 2, kk % 2]

    def strip(i):
        left = t[:, pl.ds(pl.multiple_of(i * 256, 256), 256)]
        late = i >= 4
        g8 = 2 * i + jnp.where(late, 1, 0)
        gd = 2 * i + jnp.where(late, 0, 1)
        for j in range(5):
            jj = lax.rem(i + j, 8)
            right = t[:, pl.ds(pl.multiple_of(jj * 256, 256), 256)]
            prod = lax.dot_general(
                left, right, (((0,), (0,)), ((), ())), preferred_element_type=jnp.float32
            )
            blocks = {
                (r, c): prod[r * B : r * B + B, c * B : c * B + B] for r in range(2) for c in range(2)
            }
            for (r, c), block in blocks.items():
                if 1 <= 2 * j + c - r <= 7:
                    chunk(2 * i + r, 2 * j + c - r)[pl.ds(0, B), :] = block
            if j == 0:
                chunk(gd, 0)[pl.ds(0, B), :] = jnp.where(row <= col, blocks[0, 0], blocks[1, 1])
                chunk(gd, 0)[pl.ds(B, 1), :] = jnp.sum(
                    jnp.where(row == col, blocks[1, 1], 0.0), axis=0, keepdims=True
                )
            if j == 4:
                chunk(g8, 0)[pl.ds(0, B), :] = jnp.where(late, blocks[1, 1], blocks[0, 0])

    to_sibling = []

    def gram_rows(stage):
        z = net.hop("z", STAGES[stage])
        pl.loop(2 * z, 2 * z + 2)(strip)

    def share(stage):
        z = net.hop("z", STAGES[stage])
        to_sibling.append(net.send(p.at[z, :, :, 1 - core], d2d.at[stage], net.sibling()))

    def join(stage):
        z = net.hop("z", STAGES[stage])
        to_sibling[stage].wait_recv()

        @pl.loop(0, 4)
        def _(i):
            p[z, i, :, core] += d2d[stage, i]

        for part in parts:
            part.start(stage)

    def pass_on(stage):
        for part in parts:
            part.pass_on(stage)

    def scores(z):
        s[pl.ds(512 * z, 512), :] = lax.dot_general(
            q[z].reshape(512, 2048),
            t[...],
            (((1,), (1,)), ((), ())),
            preferred_element_type=jnp.float32,
        )

    last = []

    def exchange(_):
        mine = p[zi, xi, yi, core, pl.ds(0, B), :] * scale
        turned = mine.T
        diagonal = p[zi, xi, yi, core, pl.ds(B, 1), :] * scale
        first = jnp.where(row <= col, mine, turned)
        second = jnp.where(row > col, mine, jnp.where(row < col, turned, jnp.broadcast_to(diagonal, (B, B))))
        even = odd == 0
        x[0] = jnp.where(packed, jnp.where(even, first, second), mine).reshape(8, 16, B)
        x[1] = jnp.where(packed, jnp.where(even, second, first), turned).reshape(8, 16, B)
        own_slot = jnp.where(packed, group, other)
        other_slot = jnp.where(packed, other, group)
        slots[own_slot] = x[0, k]
        for m in range(1, 8):
            to = lax.rem(k + m, 8)
            copy = pltpu.make_async_remote_copy(
                src_ref=x.at[0, to],
                dst_ref=slots.at[own_slot],
                send_sem=xsem.at[0, m],
                recv_sem=xsem.at[1, m],
                device_id=member(group, to),
                device_id_type=MESH,
            )
            copy.start()
            last.append(copy)
        for m in range(8):
            copy = pltpu.make_async_remote_copy(
                src_ref=x.at[1, m],
                dst_ref=slots.at[other_slot],
                send_sem=xsem.at[0, 8 + m],
                recv_sem=xsem.at[1, 8 + k],
                device_id=member(other, jnp.int32(m)),
                device_id_type=MESH,
            )
            copy.start()
            last.append(copy)

    gather = [gather_part(net, q, *part) for part in AG_PARTS]
    parts = [Reduce(net, p, bufs[i], *part) for i, part in enumerate(RS_PARTS)]
    reduce = [part.rest() for part in parts]
    plan = {
        "gather": lambda _: step_all(gather),
        "reduce": lambda _: step_all(reduce),
        "gram": gram_rows,
        "share": share,
        "join": join,
        "pass": pass_on,
        "scores": scores,
        "exchange": exchange,
    }

    gram_rows(0)
    gram_rows(1)
    pl.semaphore_wait(barrier, 10)
    load_q.wait()
    for step in ORDER:
        name, *at = step.split()
        plan[name](int(at[0]) if at else None)
    assert not step_all(gather) and not step_all(reduce)

    for m in range(1, 16):
        pltpu.make_async_remote_copy(
            src_ref=x.at[0, 0],
            dst_ref=slots.at[0],
            send_sem=xsem.at[0, m],
            recv_sem=xsem.at[1, m],
            device_id=net.sibling(),
            device_id_type=MESH,
        ).wait_recv()
    for c in range(16):
        g_out[:, pl.ds(c * B, B)] = slots[c]
    for copy in last + net.sent:
        copy.wait_send()


def finish(s_in, g_in, q_in, t_in, s_out, g_out, last, sem):
    done = s_in.shape[0]
    moves = [
        pltpu.make_async_copy(s_in, s_out.at[pl.ds(0, done)], sem.at[0]),
        pltpu.make_async_copy(g_in, g_out, sem.at[1]),
    ]
    for move in moves:
        move.start()
    rows = 256
    for h in range(last.shape[0] // rows):
        here = pl.ds(h * rows, rows)
        last[here, :] = lax.dot_general(
            q_in[HERE + h // 2, pl.ds(h % 2 * 2, 2)].reshape(rows, q_in.shape[-1]),
            t_in[...],
            (((1,), (1,)), ((), ())),
            preferred_element_type=jnp.float32,
        )
        move = pltpu.make_async_copy(
            last.at[here], s_out.at[pl.ds(done + h * rows, rows)], sem.at[2 + h]
        )
        move.start()
        moves.append(move)
    for move in moves:
        move.wait()


def local(scale, queries, training):
    n_rows, width = training.shape
    f32, bf16 = jnp.float32, jnp.bfloat16
    vmem, hbm = pl.BlockSpec(memory_space=pltpu.VMEM), pl.BlockSpec(memory_space=pltpu.HBM)
    scratch = [
        pltpu.VMEM((4, 4, 4, 2, CH, B), f32),
        pltpu.VMEM((4, 4, 4, CH, B), f32),
        pltpu.VMEM((2, 8, 16, B), f32),
        pltpu.VMEM((16, 16, B), f32),
    ]
    for part in RS_PARTS:
        for shapes in part_buffers(*part):
            scratch += [pltpu.VMEM(shape, f32) for shape in shapes]
    scratch += [
        pltpu.SemaphoreType.DMA((N_SEM,)),
        pltpu.SemaphoreType.DMA((N_SEM,)),
        pltpu.SemaphoreType.DMA((2, 16)),
        pltpu.SemaphoreType.DMA((6,)),
    ]
    some, gram, q, t = pl.pallas_call(
        functools.partial(kernel, scale),
        out_shape=(
            pltpu.VMEM((512 * HERE, n_rows), f32),
            pltpu.VMEM((16, 16 * B), f32),
            pltpu.VMEM((4, 4, 4, 2, 16, width), bf16),
            pltpu.VMEM((n_rows, width), bf16),
        ),
        in_specs=[hbm] * 2,
        out_specs=(vmem,) * 4,
        scratch_shapes=scratch,
        compiler_params=pltpu.CompilerParams(
            collective_id=0, has_side_effects=True, vmem_limit_bytes=24 * 2**20
        ),
        cost_estimate=pl.CostEstimate(
            flops=2 * 2048 * n_rows * 2048 * 2, bytes_accessed=20 * 2**20, transcendentals=0
        ),
    )(*(pltpu.with_memory_space_constraint(a, pltpu.HBM) for a in (queries, training)))
    return pl.pallas_call(
        finish,
        out_shape=(
            jax.ShapeDtypeStruct((2048, n_rows), f32),
            jax.ShapeDtypeStruct((16, 16 * B), f32),
        ),
        in_specs=[vmem] * 4,
        out_specs=(hbm, hbm),
        scratch_shapes=[pltpu.VMEM((512 * (4 - HERE), n_rows), f32), pltpu.SemaphoreType.DMA((10,))],
        compiler_params=pltpu.CompilerParams(vmem_limit_bytes=16 * 2**20),
    )(some, gram, q, t)


def solution(mesh):
    in_specs = (P(("blk", "grp"), None), P(("blk", "grp"), None))
    out_specs = (P(None, ("blk", "grp")), P(("blk", "grp"), None))
    return jax.shard_map(
        functools.partial(local, 1.0 / 131072),
        mesh=mesh,
        in_specs=in_specs,
        out_specs=out_specs,
        check_vma=False,
    )
```

profile of v0, /device:TPU:1, one launch (start us, length us, event | category | flops | bytes accessed | tf_op | source)
XLA Modules:
  0.0 65.7 jit_solution(763622498859934179)
XLA Ops:
  0.6 61.4 %shard_map.41 = (f32[1536,1024]{1,0:T(8,128)S(1)}, f32[16,2048]{1,0:T(8,128)S(1)}, bf16[4,4,4,2,16,2048]{5,4,3,2,1,0:T(8,128)(2,1)S(1)}, bf16[1024,2048]{1,0:T(8,128)(2,1)S(1)}) custom-call(bf16[16,2048]{1,0:T(8,128)(2,1)} %refs_0_.1, bf16[1024,2048]{1,0:T(8,128)(2,1)} %refs_1_.1), custom_call_target="tpu_custom_call" | custom-call | flops 17179869184 | bytes 20971520 | tf_op jit(solution)/shard_map/pallas_call | solution.py:489
  62.0 3.5 %shard_map.42 = (f32[2048,1024]{1,0:T(8,128)}, f32[16,2048]{1,0:T(8,128)}) custom-call(f32[1536,1024]{1,0:T(8,128)S(1)} %get-tuple-element.6.s_in, f32[16,2048]{1,0:T(8,128)S(1)} %get-tuple-element.7.g_in, bf16[4,4,4,2,16,2048]{5,4,3,2,1,0:T(8,128)(2,1)S(1)} %get-tuple-element.8.q_in, bf16[1024,2048]{1,0:T(8,128)(2,1)S(1)} %get-tuple-element.9.t_in), custom_call_target="tpu_custom_call" | custom-call | tf_op jit(solution)/shard_map/pallas_call | solution.py:507
where the time goes:
time: 65.8 us; the launch traced here: 65.7 us
  Pallas kernels  64.9 us (99%)
  between operations  0.8 us (1%)
    pallas_call x1, Pallas kernels, local(): pl.pallas_call(functools.partial(kernel, scale), out_shape=(pltpu.VMEM((5...  61.4 us
    pallas_call x1, Pallas kernels, local(): pl.pallas_call(finish, out_shape=(jax.ShapeDtypeStruct((2048, n_rows), f3...  3.49 us

commit v1 on v0

--- a/solution.py
+++ b/solution.py
@@ -30,6 +30,7 @@
     "share 3",
     "pass 0",
     "join 2",
+    "gather",
     "pass 1",
     "join 3",
     "pass 2",
@@ -38,10 +39,11 @@
     "reduce",
     "gather",
     "reduce",
-    "gather",
+    "drain 30",
     "gather",
     "reduce",
     "exchange",
+    "gather",
     "scores 0",
     "scores 1",
     "scores 2",
@@ -136,12 +138,21 @@
     for copy in first:
         copy.wait_recv()
     idx = {**idx, order[0]: ALL}
-    second = spread(order[1])
+    axis = order[1]
+    here = region(idx)
+    up, down = (net.send(here, here, net.neighbour(axis, by)) for by in (1, -1))
     third = [ahead(idx)]
     hand(idx)
     yield
-    for copy in second:
-        copy.wait_recv()
+    up.wait_recv()
+    src = halves({**idx, axis: stored(axis, net.hop(axis, -1))})[0]
+    on_up = net.send(src, src, net.neighbour(axis, 1))
+    down.wait_recv()
+    src = halves({**idx, axis: stored(axis, net.hop(axis, 1))})[1]
+    on_down = net.send(src, src, net.neighbour(axis, -1))
+    yield
+    on_up.wait_recv()
+    on_down.wait_recv()
     for by in (1, -1, 2):
         at = {**idx, order[1]: stored(order[1], net.hop(order[1], by))}
         third.append(ahead(at))
@@ -207,21 +218,24 @@
         if whole or STAGES[stage] == 3:
             self.go(stage, "own_down", self.halves(stage, -1)[0], 3, self.down)
 
-    def add(self, stage, name, ref):
-        copy, dst = self.copies[stage, name]
-        copy.wait_recv()
-        ref[...] += dst[...]
+    def add(self, ref, *arrived):
+        for at in arrived:
+            self.copies[at][0].wait_recv()
+        total = ref[...]
+        for at in arrived:
+            total = total + self.copies[at][1][...]
+        ref[...] = total
 
     def pass_on(self, stage):
         whole = self.order[0] != "z"
         via = stage if whole else STAGES.index(2)
         if whole or STAGES[stage] == 1:
             high = self.halves(stage, 1)[0]
-            self.add(via, "via_up", high)
+            self.add(high, (via, "via_up"))
             self.go(stage, "sum_up", high, 4, self.up)
         if whole or STAGES[stage] == 3:
             low = self.halves(stage, -1)[1]
-            self.add(via, "via_down", low)
+            self.add(low, (via, "via_down"))
             self.go(stage, "sum_down", low, 5, self.down)
 
     def rest(self):
@@ -229,13 +243,9 @@
         whole = order[0] != "z"
         for stage in range(4) if whole else (None,):
             mine = self.halves(stage, 0)
-            for name, h, at in (
-                ("own_up", 1, STAGES.index(1)),
-                ("sum_down", 1, STAGES.index(3)),
-                ("own_down", 0, STAGES.index(3)),
-                ("sum_up", 0, STAGES.index(1)),
-            ):
-                self.add(stage if whole else at, name, mine[h])
+            one, three = (stage, stage) if whole else (STAGES.index(1), STAGES.index(3))
+            self.add(mine[1], (one, "own_up"), (three, "sum_down"))
+            self.add(mine[0], (three, "own_down"), (one, "sum_up"))
         idx = {**{a: ALL for a in AXES}, order[0]: stored(order[0], net.at[order[0]])}
         for axis, buf in zip(order[1:], self.bufs[1:], strict=True):
             copies = [
@@ -294,9 +304,10 @@
         pl.semaphore_signal(barrier, inc=1, device_id=device, device_id_type=MESH)
 
     for axis in AXES:
+        greet(net.neighbour(axis, 2))
+    for axis in AXES:
         greet(net.neighbour(axis, 1))
         greet(net.neighbour(axis, -1))
-        greet(net.neighbour(axis, 2))
     greet(net.sibling())
     load_t.wait()
 
@@ -379,6 +390,17 @@
         own_slot = jnp.where(packed, group, other)
         other_slot = jnp.where(packed, other, group)
         slots[own_slot] = x[0, k]
+        for m in range(8):
+            copy = pltpu.make_async_remote_copy(
+                src_ref=x.at[1, m],
+                dst_ref=slots.at[other_slot],
+                send_sem=xsem.at[0, 8 + m],
+                recv_sem=xsem.at[1, 8 + k],
+                device_id=member(other, jnp.int32(m)),
+                device_id_type=MESH,
+            )
+            copy.start()
+            last.append(copy)
         for m in range(1, 8):
             to = lax.rem(k + m, 8)
             copy = pltpu.make_async_remote_copy(
@@ -391,22 +413,17 @@
             )
             copy.start()
             last.append(copy)
-        for m in range(8):
-            copy = pltpu.make_async_remote_copy(
-                src_ref=x.at[1, m],
-                dst_ref=slots.at[other_slot],
-                send_sem=xsem.at[0, 8 + m],
-                recv_sem=xsem.at[1, 8 + k],
-                device_id=member(other, jnp.int32(m)),
-                device_id_type=MESH,
-            )
-            copy.start()
-            last.append(copy)
 
     gather = [gather_part(net, q, *part) for part in AG_PARTS]
     parts = [Reduce(net, p, bufs[i], *part) for i, part in enumerate(RS_PARTS)]
     reduce = [part.rest() for part in parts]
+    def drain(kept):
+        for copy in net.sent[:-kept]:
+            copy.wait_send()
+        del net.sent[:-kept]
+
     plan = {
+        "drain": drain,
         "gather": lambda _: step_all(gather),
         "reduce": lambda _: step_all(reduce),
         "gram": gram_rows,

time: 65.8 us -> 65.4 us (level)
  no operation moved by 1% of the time
where the time goes in v1:
time: 65.4 us; the launch traced here: 65.2 us
  Pallas kernels  64.4 us (98%)
  between operations  0.8 us (1%)
    pallas_call x1, Pallas kernels, local(): pl.pallas_call(functools.partial(kernel, scale), out_shape=(pltpu.VMEM((5...  61 us
    pallas_call x1, Pallas kernels, local(): pl.pallas_call(finish, out_shape=(jax.ShapeDtypeStruct((2048, n_rows), f3...  3.49 us

profile of v1, /device:TPU:1, one launch (start us, length us, event | category | flops | bytes accessed | tf_op | source)
XLA Modules:
  0.0 65.2 jit_solution(17381947089630275909)
XLA Ops:
  0.6 61.0 %shard_map.41 = (f32[1536,1024]{1,0:T(8,128)S(1)}, f32[16,2048]{1,0:T(8,128)S(1)}, bf16[4,4,4,2,16,2048]{5,4,3,2,1,0:T(8,128)(2,1)S(1)}, bf16[1024,2048]{1,0:T(8,128)(2,1)S(1)}) custom-call(bf16[16,2048]{1,0:T(8,128)(2,1)} %refs_0_.1, bf16[1024,2048]{1,0:T(8,128)(2,1)} %refs_1_.1), custom_call_target="tpu_custom_call" | custom-call | flops 17179869184 | bytes 20971520 | tf_op jit(solution)/shard_map/pallas_call | solution.py:506
  61.6 3.5 %shard_map.42 = (f32[2048,1024]{1,0:T(8,128)}, f32[16,2048]{1,0:T(8,128)}) custom-call(f32[1536,1024]{1,0:T(8,128)S(1)} %get-tuple-element.6.s_in, f32[16,2048]{1,0:T(8,128)S(1)} %get-tuple-element.7.g_in, bf16[4,4,4,2,16,2048]{5,4,3,2,1,0:T(8,128)(2,1)S(1)} %get-tuple-element.8.q_in, bf16[1024,2048]{1,0:T(8,128)(2,1)S(1)} %get-tuple-element.9.t_in), custom_call_target="tpu_custom_call" | custom-call | tf_op jit(solution)/shard_map/pallas_call | solution.py:524

commit v2 on v1

--- a/solution.py
+++ b/solution.py
@@ -35,7 +35,6 @@
     "join 3",
     "pass 2",
     "pass 3",
-    "gather",
     "reduce",
     "gather",
     "reduce",
@@ -365,8 +364,10 @@
             part.start(stage)
 
     def pass_on(stage):
-        for part in parts:
-            part.pass_on(stage)
+        for i in (2, 0, 1):
+            parts[i].pass_on(stage)
+            if stage == (2 if i == 0 else 3):
+                next(gather[i])
 
     def scores(z):
         s[pl.ds(512 * z, 512), :] = lax.dot_general(

time: 65.4 us -> 65.1 us (level)
  no operation moved by 1% of the time
where the time goes in v2:
time: 65.1 us; the launch traced here: 65 us
  Pallas kernels  64.2 us (99%)
  between operations  0.8 us (1%)
    pallas_call x1, Pallas kernels, local(): pl.pallas_call(functools.partial(kernel, scale), out_shape=(pltpu.VMEM((5...  60.7 us
    pallas_call x1, Pallas kernels, local(): pl.pallas_call(finish, out_shape=(jax.ShapeDtypeStruct((2048, n_rows), f3...  3.49 us

profile of v2, /device:TPU:1, one launch (start us, length us, event | category | flops | bytes accessed | tf_op | source)
XLA Modules:
  0.0 65.0 jit_solution(17303787360308741057)
XLA Ops:
  0.6 60.7 %shard_map.41 = (f32[1536,1024]{1,0:T(8,128)S(1)}, f32[16,2048]{1,0:T(8,128)S(1)}, bf16[4,4,4,2,16,2048]{5,4,3,2,1,0:T(8,128)(2,1)S(1)}, bf16[1024,2048]{1,0:T(8,128)(2,1)S(1)}) custom-call(bf16[16,2048]{1,0:T(8,128)(2,1)} %refs_0_.1, bf16[1024,2048]{1,0:T(8,128)(2,1)} %refs_1_.1), custom_call_target="tpu_custom_call" | custom-call | flops 17179869184 | bytes 20971520 | tf_op jit(solution)/shard_map/pallas_call | solution.py:507
  61.3 3.5 %shard_map.42 = (f32[2048,1024]{1,0:T(8,128)}, f32[16,2048]{1,0:T(8,128)}) custom-call(f32[1536,1024]{1,0:T(8,128)S(1)} %get-tuple-element.6.s_in, f32[16,2048]{1,0:T(8,128)S(1)} %get-tuple-element.7.g_in, bf16[4,4,4,2,16,2048]{5,4,3,2,1,0:T(8,128)(2,1)S(1)} %get-tuple-element.8.q_in, bf16[1024,2048]{1,0:T(8,128)(2,1)S(1)} %get-tuple-element.9.t_in), custom_call_target="tpu_custom_call" | custom-call | tf_op jit(solution)/shard_map/pallas_call | solution.py:525

commit v3 on v1

--- a/solution.py
+++ b/solution.py
@@ -461,9 +461,10 @@
 def finish(s_in, g_in, q_in, t_in, s_out, g_out, last, sem):
     done = s_in.shape[0]
     moves = [
-        pltpu.make_async_copy(s_in, s_out.at[pl.ds(0, done)], sem.at[0]),
-        pltpu.make_async_copy(g_in, g_out, sem.at[1]),
+        pltpu.make_async_copy(s_in.at[pl.ds(i * 512, 512)], s_out.at[pl.ds(i * 512, 512)], sem.at[4 + i])
+        for i in range(done // 512)
     ]
+    moves.append(pltpu.make_async_copy(g_in, g_out, sem.at[1]))
     for move in moves:
         move.start()
     rows = 256
@@ -529,7 +530,7 @@
         ),
         in_specs=[vmem] * 4,
         out_specs=(hbm, hbm),
-        scratch_shapes=[pltpu.VMEM((512 * (4 - HERE), n_rows), f32), pltpu.SemaphoreType.DMA((10,))],
+        scratch_shapes=[pltpu.VMEM((512 * (4 - HERE), n_rows), f32), pltpu.SemaphoreType.DMA((16,))],
         compiler_params=pltpu.CompilerParams(vmem_limit_bytes=16 * 2**20),
     )(some, gram, q, t)
 

time: 65.4 us -> 65.4 us (level)
  no operation moved by 1% of the time
where the time goes in v3:
time: 65.4 us; the launch traced here: 65.2 us
  Pallas kernels  64.4 us (98%)
  between operations  0.8 us (1%)
    pallas_call x1, Pallas kernels, local(): pl.pallas_call(functools.partial(kernel, scale), out_shape=(pltpu.VMEM((5...  61 us
    pallas_call x1, Pallas kernels, local(): pl.pallas_call(finish, out_shape=(jax.ShapeDtypeStruct((2048, n_rows), f3...  3.48 us

profile of v3, /device:TPU:1, one launch (start us, length us, event | category | flops | bytes accessed | tf_op | source)
XLA Modules:
  0.0 65.2 jit_solution(4127262226004695885)
XLA Ops:
  0.6 61.0 %shard_map.41 = (f32[1536,1024]{1,0:T(8,128)S(1)}, f32[16,2048]{1,0:T(8,128)S(1)}, bf16[4,4,4,2,16,2048]{5,4,3,2,1,0:T(8,128)(2,1)S(1)}, bf16[1024,2048]{1,0:T(8,128)(2,1)S(1)}) custom-call(bf16[16,2048]{1,0:T(8,128)(2,1)} %refs_0_.1, bf16[1024,2048]{1,0:T(8,128)(2,1)} %refs_1_.1), custom_call_target="tpu_custom_call" | custom-call | flops 17179869184 | bytes 20971520 | tf_op jit(solution)/shard_map/pallas_call | solution.py:507
  61.6 3.5 %shard_map.42 = (f32[2048,1024]{1,0:T(8,128)}, f32[16,2048]{1,0:T(8,128)}) custom-call(f32[1536,1024]{1,0:T(8,128)S(1)} %get-tuple-element.6.s_in, f32[16,2048]{1,0:T(8,128)S(1)} %get-tuple-element.7.g_in, bf16[4,4,4,2,16,2048]{5,4,3,2,1,0:T(8,128)(2,1)S(1)} %get-tuple-element.8.q_in, bf16[1024,2048]{1,0:T(8,128)(2,1)S(1)} %get-tuple-element.9.t_in), custom_call_target="tpu_custom_call" | custom-call | tf_op jit(solution)/shard_map/pallas_call | solution.py:525
